TPU v7x, 256 devices: a whole 4x4x8 slice. The times are simulated.
256 devices in a mesh: angle: 16 (over y, x), panel: 16 (over z, core).
Axes of the slice: x: 4, y: 4, z: 8, core: 2. Of those that a mesh axis runs over, the one named last changes fastest.
Arguments:
- measured: bfloat16 [512, 512, 1024], P(('angle', 'panel')), may hold values from 0.099609375 to 1
- predicted: bfloat16 [512, 512, 1024], P(('angle', 'panel')), may hold values from 0 to 2
- slice_filter: bfloat16 [512, 512], replicated, may hold values from -0.25 to 0.25
- column_filter: bfloat16 [1024, 1024], replicated, may hold values from -0.1875 to 0.1875
- volume: float32 [512, 32768], P('angle', 'panel'), may hold values from 0 to 1
- tiles: bfloat16 [3072, 128, 128], P('panel'), may hold values from -0.5 to 0.5
- tile_ray: int32 [3072], P('panel'), may hold values from 0 to 255
- tile_vox: int32 [3072], P('panel'), may hold values from 0 to 255
- live_tiles: int32 [16], P('panel'), may hold values from 1 to 192, as said below
Outputs:
- updated_volume: float32 [512, 32768], P('angle', 'panel')
- projected: bfloat16 [512, 512, 1024], P(('angle', 'panel'))
Inputs may be any that keep to these rules, and one draw needn't show every extreme that they name: live_tiles[p] counts the tile slots of panel p that are used, from the first slot on; at least one panel uses all 192 slots.
All inputs are finite; a program needn't handle non-finite values.
Results may differ from a plain program's by a relative error of at most 0.0065.
Values may be sent and summed in bfloat16 or wider, within the bound.
A program may use at most 128 MiB of HBM per device.

v0:
```python
import math

import jax
import jax.numpy as jnp
from jax import lax
from jax.sharding import Mesh
from jax.sharding import PartitionSpec as P

PANEL = ("panel_0", "panel_1")
ANGLE_PANEL = ("angle", "panel_0", "panel_1")


step_size = 0.1


def gathered_by_axis(x, axes, dim):
    if not axes:
        return x
    nearer = lax.all_gather(x, axes[-1], axis=dim, tiled=True)
    return gathered_by_axis(nearer, axes[:-1], dim)


def per_device(
    measured, predicted, slice_filter, column_filter, volume, tiles, tile_ray, tile_vox, live_tiles
):
    detector_cols = measured.shape[2]
    bright = jnp.exp(-predicted.astype(jnp.float32))
    misfit = ((measured.astype(jnp.float32) - bright) * bright).astype(jnp.bfloat16)
    across = jnp.dot(
        misfit.reshape(-1, detector_cols), column_filter, preferred_element_type=jnp.float32
    )
    across = across.astype(jnp.bfloat16).reshape(misfit.shape)
    filtered = jnp.einsum(
        "ij,ajc->aic", slice_filter, across, preferred_element_type=jnp.float32
    ).astype(jnp.bfloat16)
    gathered = lax.all_to_all(filtered, "angle", split_axis=1, concat_axis=0, tiled=True)
    angle_count = gathered.shape[0]
    slice_rows = gathered.shape[1]
    col_blocks = detector_cols // 128
    ray_grid = gathered.reshape(angle_count, slice_rows, col_blocks, 128)
    vox_dev = volume.shape[1]
    voxel_count = vox_dev * lax.axis_size(PANEL)
    voxel_blocks = voxel_count // 128
    tile_slots = tiles.shape[0]
    tile_block = math.gcd(tile_slots, 32)
    live_count = live_tiles[0]
    loop_turns = tile_slots // tile_block

    def slot_pieces(turn_index):
        first_tile = turn_index * tile_block
        ray_ids = lax.dynamic_slice_in_dim(tile_ray, first_tile, tile_block)
        vox_ids = lax.dynamic_slice_in_dim(tile_vox, first_tile, tile_block)
        tile_piece = lax.dynamic_slice_in_dim(tiles, first_tile, tile_block, 0)
        active = first_tile + jnp.arange(tile_block) < live_count
        return (ray_ids, vox_ids, tile_piece, active)

    def back_turn(turn_index, summed):
        ray_ids, vox_ids, tile_piece, active = slot_pieces(turn_index)
        picked = ray_grid[ray_ids // col_blocks, :, ray_ids % col_blocks, :]
        contrib = jnp.einsum("tsr,trv->stv", picked, tile_piece, preferred_element_type=jnp.float32)
        contrib = jnp.where(active[None, :, None], contrib, jnp.float32(0.0))
        return summed.at[:, vox_ids, :].add(contrib)

    gradient = lax.fori_loop(
        0, loop_turns, back_turn, jnp.zeros((slice_rows, voxel_blocks, 128), jnp.float32)
    )
    gradient = gradient.reshape(slice_rows, voxel_count)
    grad_share = lax.psum_scatter(
        gradient.astype(jnp.bfloat16), PANEL, scatter_dimension=1, tiled=True
    ).astype(jnp.float32)
    new_share = jnp.clip(volume + step_size * grad_share, 0.0, 1.0)
    voxels = gathered_by_axis(new_share.astype(jnp.bfloat16), PANEL, 1)
    voxel_grid = voxels.reshape(slice_rows, voxel_blocks, 128)

    def fore_turn(turn_index, summed):
        ray_ids, vox_ids, tile_piece, active = slot_pieces(turn_index)
        picked = voxel_grid[:, vox_ids, :]
        contrib = jnp.einsum("stv,trv->tsr", picked, tile_piece, preferred_element_type=jnp.float32)
        contrib = jnp.where(active[:, None, None], contrib, jnp.float32(0.0))
        return summed.at[ray_ids // col_blocks, :, ray_ids % col_blocks, :].add(contrib)

    rays_sum = lax.fori_loop(
        0, loop_turns, fore_turn, jnp.zeros((angle_count, slice_rows, col_blocks, 128), jnp.float32)
    )
    forward_rays = rays_sum.astype(jnp.bfloat16).reshape(angle_count, slice_rows, detector_cols)
    returned = lax.all_to_all(forward_rays, "angle", split_axis=0, concat_axis=1, tiled=True)
    return (new_share, returned)


def solution(mesh):
    split = Mesh(mesh.devices.reshape(mesh.shape["angle"], 8, 2), ("angle", "panel_0", "panel_1"))
    return jax.shard_map(
        per_device,
        mesh=split,
        in_specs=(
            P(ANGLE_PANEL, None, None),
            P(ANGLE_PANEL, None, None),
            P(),
            P(),
            P("angle", PANEL),
            P(PANEL, None, None),
            P(PANEL),
            P(PANEL),
            P(PANEL),
        ),
        out_specs=(P("angle", PANEL), P(ANGLE_PANEL, None, None)),
        check_vma=False,
    )
```

profile of v0, /device:TPU:1, one launch (start us, length us, event | category | flops | bytes accessed | tf_op | source)
XLA Modules:
  0.0 328.9 jit_solution(895395324277027932)
XLA Ops:
  7.2 3.4 %fusion.15 = bf16[2,512,1024]{2,1,0:T(8,128)(2,1)S(1)} fusion(bf16[2,512,1024]{2,1,0:T(8,128)(2,1)} %param.14, bf16[2,512,1024]{2,1,0:T(8,128)(2,1)} %param.13), kind=kLoop, calls=%fused_computation.44 | loop fusion | flops 6291456 | bytes 6291456 | tf_op jit(solution)/shard_map/convert_element_type | solution.py:28
  15.6 6.3 %copy.30 = bf16[2,512,1024]{2,0,1:T(2,128)(2,1)} copy(bf16[2,512,1024]{1,2,0:T(8,128)(2,1)} %convert_bitcast_fusion.2) | data formatting | bytes 4194304 | tf_op jit(solution)/shard_map/convert_element_type | solution.py:35
  21.9 7.6 %all-to-all-start = ((bf16[2,512,1024]{2,0,1:T(2,128)(2,1)}), bf16[2,512,1024]{2,0,1:T(2,128)(2,1)}, u32[]{:S(2)}, u32[]{:S(2)}) async-start(bf16[2,512,1024]{2,0,1:T(2,128)(2,1)} %copy.30), calls=%async_computation | async-start | bytes 4194304 | tf_op jit(solution)/shard_map/all_to_all | solution.py:36
  29.6 30.5 %all-to-all-done = bf16[2,512,1024]{2,0,1:T(2,128)(2,1)} async-done(((bf16[2,512,1024]{2,0,1:T(2,128)(2,1)}), bf16[2,512,1024]{2,0,1:T(2,128)(2,1)}, u32[]{:S(2)}, u32[]{:S(2)}) %all-to-all-start) | async-done | bytes 2097184 | tf_op jit(solution)/shard_map/all_to_all | solution.py:36
  67.5 53.5 %while.30 = (s32[]{:T(128)}, f32[32,256,128]{2,0,1:T(8,128)}, s32[192]{0:T(256)S(1)}, s32[]{:T(128)}, bf16[192,128,128]{2,1,0:T(8,128)(2,1)}, /*index=5*/s32[192...) while((s32[]{:T(128)}, f32[32,256,128]{2,0,1:T(8,128)}, ...), condition=%wide.region_2.3_spmd, body=%wide.region_0.2_spmd.sunk | while | flops 33817700 | bytes 3933291 | solution.py:64
  72.1 4.3 %scatter_fusion = f32[32,256,128]{2,0,1:T(8,128)} fusion(f32[32,256,128]{2,0,1:T(8,128)} %get-tuple-element.531, s32[32]{0:T(128)S(1)} %get-tuple-element.510, f32[32,32,128]{2,1,0:T(8,128)S(1)} %fusion.31), kind=kCustom, calls=%fused_computation.2.clone.1 | custom fusion | flops 131072 | bytes 1572992 | tf_op jit(solution)/shard_map/while/body/eval_jaxpr/scatter-add | solution.py:62
  81.0 4.3 %scatter_fusion = f32[32,256,128]{2,0,1:T(8,128)} fusion(f32[32,256,128]{2,0,1:T(8,128)} %get-tuple-element.531, s32[32]{0:T(128)S(1)} %get-tuple-element.510, f32[32,32,128]{2,1,0:T(8,128)S(1)} %fusion.31), kind=kCustom, calls=%fused_computation.2.clone.1 | custom fusion | flops 131072 | bytes 1572992 | tf_op jit(solution)/shard_map/while/body/eval_jaxpr/scatter-add | solution.py:62
  89.9 4.3 %scatter_fusion = f32[32,256,128]{2,0,1:T(8,128)} fusion(f32[32,256,128]{2,0,1:T(8,128)} %get-tuple-element.531, s32[32]{0:T(128)S(1)} %get-tuple-element.510, f32[32,32,128]{2,1,0:T(8,128)S(1)} %fusion.31), kind=kCustom, calls=%fused_computation.2.clone.1 | custom fusion | flops 131072 | bytes 1572992 | tf_op jit(solution)/shard_map/while/body/eval_jaxpr/scatter-add | solution.py:62
  98.8 4.3 %scatter_fusion = f32[32,256,128]{2,0,1:T(8,128)} fusion(f32[32,256,128]{2,0,1:T(8,128)} %get-tuple-element.531, s32[32]{0:T(128)S(1)} %get-tuple-element.510, f32[32,32,128]{2,1,0:T(8,128)S(1)} %fusion.31), kind=kCustom, calls=%fused_computation.2.clone.1 | custom fusion | flops 131072 | bytes 1572992 | tf_op jit(solution)/shard_map/while/body/eval_jaxpr/scatter-add | solution.py:62
  107.8 4.3 %scatter_fusion = f32[32,256,128]{2,0,1:T(8,128)} fusion(f32[32,256,128]{2,0,1:T(8,128)} %get-tuple-element.531, s32[32]{0:T(128)S(1)} %get-tuple-element.510, f32[32,32,128]{2,1,0:T(8,128)S(1)} %fusion.31), kind=kCustom, calls=%fused_computation.2.clone.1 | custom fusion | flops 131072 | bytes 1572992 | tf_op jit(solution)/shard_map/while/body/eval_jaxpr/scatter-add | solution.py:62
  116.7 4.3 %scatter_fusion = f32[32,256,128]{2,0,1:T(8,128)} fusion(f32[32,256,128]{2,0,1:T(8,128)} %get-tuple-element.531, s32[32]{0:T(128)S(1)} %get-tuple-element.510, f32[32,32,128]{2,1,0:T(8,128)S(1)} %fusion.31), kind=kCustom, calls=%fused_computation.2.clone.1 | custom fusion | flops 131072 | bytes 1572992 | tf_op jit(solution)/shard_map/while/body/eval_jaxpr/scatter-add | solution.py:62
  121.0 3.7 %copy_bitcast_fusion.1 = bf16[32,32768]{1,0:T(8,128)(2,1)} fusion(f32[32,256,128]{2,0,1:T(8,128)} %get-tuple-element.360), kind=kLoop, calls=%fused_computation.46 | loop fusion | flops 1048576 | bytes 6291456 | tf_op jit(solution)/shard_map/convert_element_type | solution.py:69
  124.8 57.4 %reduce-scatter.2.cloned.1.call-done = bf16[32,2048]{1,0:T(8,128)(2,1)} async-done(((bf16[32,32768]{1,0:T(8,128)(2,1)}), bf16[32,2048]{1,0:T(8,128)(2,1)}) %reduce-scatter.2.cloned.1.call-update) | async-done | bytes 131088 | tf_op jit(solution)/shard_map/reduce_scatter | solution.py:68
  183.8 5.4 %all_gather.6 = bf16[32,4096]{1,0:T(8,128)(2,1)} all-gather(bf16[32,2048]{1,0:T(8,128)(2,1)S(1)} %get-tuple-element.425), channel_id=1, replica_groups=mesh['angle'=16,'panel_0'=8,'panel_1'=2] {'panel_1'}, dimensions={1}, use_global_device_ids=true | all-gather | bytes 393216 | tf_op jit(solution)/shard_map/all_gather | solution.py:19
  189.2 35.8 %all-gather.2.cloned.1.call-done = bf16[32,32768]{1,0:T(8,128)(2,1)} async-done(((bf16[32,4096]{1,0:T(8,128)(2,1)}), bf16[32,32768]{1,0:T(8,128)(2,1)}) %all-gather.2.cloned.1.call-update) | async-done | bytes 2097168 | tf_op jit(solution)/shard_map/all_gather | solution.py:19
  225.0 3.3 copy_bitcast_fusion.2
  230.7 56.9 %while.31 = (s32[]{:T(128)}, f32[32,32,8,128]{3,1,2,0:T(8,128)}, s32[192]{0:T(256)S(1)}, s32[]{:T(128)}, s32[192]{0:T(256)S(1)}, /*index=5*/bf16[32,256,128]{2,0...) while((s32[]{:T(128)}, f32[32,32,8,128]{3,1,2,0:T(8,128)}, ...), condition=%wide.region_6.7_spmd, body=%wide.region_4.6_spmd.sunk | while | flops 33818852 | bytes 3937519 | solution.py:82
  235.6 4.6 %scatter_fusion.1 = f32[32,32,8,128]{3,1,2,0:T(8,128)} fusion(f32[32,32,8,128]{3,1,2,0:T(8,128)} %get-tuple-element.564, s32[32]{0:T(128)S(1)} %fusion.34, f32[32,32,128]{2,1,0:T(8,128)S(1)} %convolution_select_fusion.3), kind=kCustom, calls=%fused_computation.3.clone.1 | custom fusion | flops 131072 | bytes 1573120 | tf_op jit(solution)/shard_map/while/body/eval_jaxpr/scatter-add | solution.py:80
  245.1 4.6 %scatter_fusion.1 = f32[32,32,8,128]{3,1,2,0:T(8,128)} fusion(f32[32,32,8,128]{3,1,2,0:T(8,128)} %get-tuple-element.564, s32[32]{0:T(128)S(1)} %fusion.34, f32[32,32,128]{2,1,0:T(8,128)S(1)} %convolution_select_fusion.3), kind=kCustom, calls=%fused_computation.3.clone.1 | custom fusion | flops 131072 | bytes 1573120 | tf_op jit(solution)/shard_map/while/body/eval_jaxpr/scatter-add | solution.py:80
  254.6 4.6 %scatter_fusion.1 = f32[32,32,8,128]{3,1,2,0:T(8,128)} fusion(f32[32,32,8,128]{3,1,2,0:T(8,128)} %get-tuple-element.564, s32[32]{0:T(128)S(1)} %fusion.34, f32[32,32,128]{2,1,0:T(8,128)S(1)} %convolution_select_fusion.3), kind=kCustom, calls=%fused_computation.3.clone.1 | custom fusion | flops 131072 | bytes 1573120 | tf_op jit(solution)/shard_map/while/body/eval_jaxpr/scatter-add | solution.py:80
  264.1 4.6 %scatter_fusion.1 = f32[32,32,8,128]{3,1,2,0:T(8,128)} fusion(f32[32,32,8,128]{3,1,2,0:T(8,128)} %get-tuple-element.564, s32[32]{0:T(128)S(1)} %fusion.34, f32[32,32,128]{2,1,0:T(8,128)S(1)} %convolution_select_fusion.3), kind=kCustom, calls=%fused_computation.3.clone.1 | custom fusion | flops 131072 | bytes 1573120 | tf_op jit(solution)/shard_map/while/body/eval_jaxpr/scatter-add | solution.py:80
  273.6 4.6 %scatter_fusion.1 = f32[32,32,8,128]{3,1,2,0:T(8,128)} fusion(f32[32,32,8,128]{3,1,2,0:T(8,128)} %get-tuple-element.564, s32[32]{0:T(128)S(1)} %fusion.34, f32[32,32,128]{2,1,0:T(8,128)S(1)} %convolution_select_fusion.3), kind=kCustom, calls=%fused_computation.3.clone.1 | custom fusion | flops 131072 | bytes 1573120 | tf_op jit(solution)/shard_map/while/body/eval_jaxpr/scatter-add | solution.py:80
  283.1 4.6 %scatter_fusion.1 = f32[32,32,8,128]{3,1,2,0:T(8,128)} fusion(f32[32,32,8,128]{3,1,2,0:T(8,128)} %get-tuple-element.564, s32[32]{0:T(128)S(1)} %fusion.34, f32[32,32,128]{2,1,0:T(8,128)S(1)} %convolution_select_fusion.3), kind=kCustom, calls=%fused_computation.3.clone.1 | custom fusion | flops 131072 | bytes 1573120 | tf_op jit(solution)/shard_map/while/body/eval_jaxpr/scatter-add | solution.py:80
  290.2 30.4 %all_to_all.33 = bf16[32,32,1024]{2,1,0:T(8,128)(2,1)S(1)} all-to-all(bf16[32,32,1024]{2,1,0:T(8,128)(2,1)S(1)} %copy_bitcast_fusion), channel_id=1, replica_groups=mesh['angle'=16,'panel_0'=8,'panel_1'=2] {'angle'}, dimensions={0} | all-to-all | bytes 4194304 | tf_op jit(solution)/shard_map/all_to_all | solution.py:86
  (85 shorter events, 77.7 us)
Async XLA Ops:
  7.2 3.4 %copy-start = (bf16[1024,1024]{1,0:T(8,128)(2,1)S(1)}, bf16[1024,1024]{1,0:T(8,128)(2,1)}, u32[]{:S(2)}) copy-start(bf16[1024,1024]{1,0:T(8,128)(2,1)} %param.16) | copy-start | bytes 6291460
  10.6 2.4 copy-start.4
  21.9 38.2 %all-to-all-start = ((bf16[2,512,1024]{2,0,1:T(2,128)(2,1)}), bf16[2,512,1024]{2,0,1:T(2,128)(2,1)}, u32[]{:S(2)}, u32[]{:S(2)}) async-start(bf16[2,512,1024]{2,0,1:T(2,128)(2,1)} %copy.30), calls=%async_computation | async-start | bytes 4194304 | tf_op jit(solution)/shard_map/all_to_all | solution.py:36
  29.5 152.6 %reduce-scatter.2.cloned.1.call-start = ((), (), s32[]{:S(2)}) async-start(), calls=%async_computation.3 | async-start | bytes 2228224 | tf_op jit(solution)/shard_map/reduce_scatter | solution.py:68
  65.0 2.5 copy-start.2
  65.0 2.5 copy-start.3
  124.7 57.4 %copy-start.1 = (f32[32,2048]{1,0:T(8,128)S(1)}, f32[32,2048]{1,0:T(8,128)}, u32[]{:S(2)}) copy-start(f32[32,2048]{1,0:T(8,128)} %param.17) | copy-start | bytes 786436
  124.8 100.2 %all-gather.2.cloned.1.call-start = ((), (), s32[]{:S(2)}) async-start(), calls=%async_computation.4 | async-start | bytes 2359296 | tf_op jit(solution)/shard_map/all_gather | solution.py:19
Sparse Core Ops, SparseCore 0:
  124.9 57.2 reduce-scatter.1
  189.3 35.5 all-gather.1
where the time goes:
time: 335 us; the launch traced here: 329 us
  waiting for transfers between devices  124 us (37%)
  other arithmetic  73.9 us (22%)
  local copies, waits for them, and re-layouts  47.6 us (14%)
  blocking collectives  35.8 us (11%)
  matrix products  25.9 us (8%)
  between operations  14.1 us (4%)
  starting transfers between devices  7.72 us (2%)
    reduce_scatter x1, waiting for transfers between devices, per_device(): lax.psum_scatter(gradient.astype(jnp.bfloat16), PANEL, scatter_dimension=...  57.4 us
    all_gather x1, waiting for transfers between devices, gathered_by_axis(): nearer = lax.all_gather(x, axes[-1], axis=dim, tiled=True)  35.8 us
    all_to_all x1, waiting for transfers between devices, per_device(): lax.all_to_all(filtered, 'angle', split_axis=1, concat_axis=0, tiled=True)  30.5 us
    all_to_all x1, blocking collectives, per_device(): lax.all_to_all(forward_rays, 'angle', split_axis=0, concat_axis=1, tiled=...  30.4 us
    scatter-add x6, other arithmetic, fore_turn(): summed.at[ray_ids // col_blocks, :, ray_ids % col_blocks, :].add(contrib)  27.4 us
    scatter-add x6, other arithmetic, back_turn(): return summed.at[:, vox_ids, :].add(contrib)  25.8 us
    gather x6, local copies, waits for them, and re-layouts, back_turn(): picked = ray_grid[ray_ids // col_blocks, :, ray_ids % col_blocks, :]  13.5 us
    gather x6, local copies, waits for them, and re-layouts, fore_turn(): picked = voxel_grid[:, vox_ids, :]  13.2 us
  transfers between devices with their start and end apart: 3, of which 3 were waited for; matrix products, arithmetic and copies ran while one was open for 0% of the time, Pallas kernels for 0%

commit v1 on v0

v1 whole, which is shorter than its diff:
```python
import functools

import jax
import jax.numpy as jnp
from jax import lax
from jax.experimental import pallas as pl
from jax.experimental.pallas import tpu as pltpu
from jax.sharding import PartitionSpec as P

MESH = pl.DeviceIdType.MESH
BF = jnp.bfloat16
F32 = jnp.float32
I32 = jnp.int32
PLANE = 16
NZ = 8
SLOTS = 192
UNROLL = 32
STEP_SIZE = 0.1
NC = 2
R = 32 // NC


def kernel(
    measured, predicted, sfilt, cfilt, volume, tiles_hbm, ray_ref, vox_ref, live_ref,
    new_out, proj_out,
    m_v, p_v, sf_v, cf_v, vol_v, tiles, misfit, across, newvol,
    keys, idx_v, idx, *rest,
):
    names = (
        "filt", "gath", "slots", "sib_out", "sib_in", "part", "near", "far", "half", "mid", "mid2",
        "vox", "fslots", "stage",
    )
    per_chunk = len(names)
    bufs = [dict(zip(names, rest[c * per_chunk:(c + 1) * per_chunk])) for c in range(NC)]
    (in_sem, idx_sem, a_send, a_recv, sib_send, sib_recv, rs_send, rs_recv,
     ag_send, ag_recv, c_send, c_recv, loc_sem) = rest[NC * per_chunk:]

    a = lax.axis_index("angle")
    pan = lax.axis_index("panel")
    z = pan // 2
    core = pan % 2
    ax, ay = a % 4, a // 4

    def plane_peer(i):
        return ((ay + i // 4) % 4) * 4 + (ax + i) % 4

    def along_z(dz):
        return {"panel": ((z + dz + NZ) % NZ) * 2 + core}

    sibling = {"panel": z * 2 + (1 - core)}

    loads = [
        pltpu.make_async_copy(src, dst, in_sem.at[i])
        for i, (src, dst) in enumerate((
            (predicted.at[0], p_v.at[0]), (measured.at[0], m_v.at[0]), (cfilt, cf_v), (sfilt, sf_v),
            (predicted.at[1], p_v.at[1]), (measured.at[1], m_v.at[1]), (tiles_hbm, tiles), (volume, vol_v),
        ))
    ]
    for load in loads:
        load.start()

    barrier = pltpu.get_barrier_semaphore()

    @pl.loop(1, PLANE)
    def _(i):
        pl.semaphore_signal(barrier, inc=1, device_id={"angle": plane_peer(i)}, device_id_type=MESH)

    for peer in (sibling, along_z(1), along_z(-1), along_z(2), along_z(-2)):
        pl.semaphore_signal(barrier, inc=1, device_id=peer, device_id_type=MESH)

    def misfit_of(k):
        @pl.loop(0, 8)
        def _(i):
            rows = pl.ds(pl.multiple_of(i * 64, 64), 64)
            bright = jnp.exp(-p_v[k, rows, :].astype(F32))
            misfit[rows, :] = ((m_v[k, rows, :].astype(F32) - bright) * bright).astype(BF)

    def across_of(k):
        @pl.loop(0, 4)
        def _(n):
            columns = pl.ds(pl.multiple_of(n * 256, 256), 256)
            across[k, n] = jnp.dot(misfit[...], cf_v[:, columns], preferred_element_type=F32).astype(BF)

    def filter_of(c, k):
        filt = bufs[c]["filt"]

        @pl.loop(0, 4)
        def _(n):
            rows = sf_v[:, c].reshape(PLANE * R, 512)
            out = jnp.dot(rows, across[k, n], preferred_element_type=F32).astype(BF)
            for d in range(PLANE):
                for j in range(2):
                    filt[d * 16 + k * 8 + n * 2 + j] = out[d * R:(d + 1) * R, j * 128:(j + 1) * 128]

    def send_filtered(c):
        filt, gath = bufs[c]["filt"], bufs[c]["gath"]

        @pl.loop(1, PLANE)
        def _(i):
            peer = plane_peer(i)
            pltpu.make_async_remote_copy(
                src_ref=filt.at[pl.ds(peer * 16, 16)],
                dst_ref=gath.at[pl.ds(a * 16, 16)],
                send_sem=a_send.at[c], recv_sem=a_recv.at[c],
                device_id={"angle": peer}, device_id_type=MESH,
            ).start()

        gath[pl.ds(a * 16, 16)] = filt[pl.ds(a * 16, 16)]

    def wait_bytes(ref, sem):
        pltpu.make_async_copy(ref, ref, sem).wait()

    def remote(src, dst, send, recv, device):
        pltpu.make_async_remote_copy(
            src_ref=src, dst_ref=dst, send_sem=send, recv_sem=recv, device_id=device, device_id_type=MESH
        ).start()

    def order_tiles():
        row = lax.broadcasted_iota(I32, (256, 256), 0)
        col = lax.broadcasted_iota(I32, (256, 256), 1)
        dead = 256
        keys[...] = jnp.full((8, 256), dead, I32)
        keys[0:1, 0:SLOTS] = vox_ref[...]
        keys[1:2, 0:SLOTS] = ray_ref[...]
        live = live_ref[0]

        def down(x):
            return jnp.sum(x, axis=0, keepdims=True)

        def spread(x):
            return jnp.broadcast_to(x, (256, 256))

        def one(main, other, at, address):
            main_row = spread(main)
            main_row = jnp.where(col < live, main_row, dead)
            main_col = main_row.T
            other_col = spread(other).T
            same_before = ((main_col == main_row) & (row < col)).astype(I32)
            before = same_before + (main_col < main_row).astype(I32)
            rank_col = spread(down(before)).T
            repeat_col = spread((down(same_before) > 0).astype(I32)).T
            placed = (rank_col == col).astype(I32)
            idx_v[at:at + 1, :] = down(placed * row)
            idx_v[at + 1:at + 2, :] = address(down(placed * other_col))
            idx_v[at + 2:at + 3, :] = down(placed * repeat_col)
            through = down((main_col <= col).astype(I32)) - 1
            present = down((main_col == col).astype(I32)) > 0
            idx_v[at + 3:at + 4, :] = jnp.where(present, through, SLOTS)

        def voxel_address(v):
            block_z, block_core = (v >> 5) & 7, (v >> 4) & 1
            return block_core * 128 + ((block_z - z + 10) & 7) * 16 + (v & 15)

        one(keys[0:1, :], keys[1:2, :], 0, lambda r: r & 255)
        one(keys[1:2, :], keys[0:1, :], 4, voxel_address)
        move = pltpu.make_async_copy(idx_v, idx, idx_sem)
        move.start()
        move.wait()

    def tile_sums(source, slots, at, transposed):
        slots[SLOTS] = jnp.zeros((R, 128), BF)
        blank = jnp.zeros((R, 128), BF)
        joined = 0 if transposed else 1
        contract = (((1,), (1,)), ((), ())) if transposed else (((1,), (0,)), ((), ()))

        def four(j, acc):
            ts = [tiles[idx[at, j + i]] for i in range(4)]
            xs = [source[idx[at + 1, j + i]] for i in range(4)]
            left = jnp.concatenate(
                [jnp.concatenate([xs[0], blank], 1), jnp.concatenate([xs[1], blank], 1),
                 jnp.concatenate([blank, xs[2]], 1), jnp.concatenate([blank, xs[3]], 1)], 0)
            right = jnp.concatenate(
                [jnp.concatenate(ts[:2], joined), jnp.concatenate(ts[2:], joined)], 1 - joined)
            out = lax.dot_general(left, right, contract, preferred_element_type=F32)
            for i in range(4):
                lane = (i % 2) * 128
                term = out[i * R:(i + 1) * R, lane:lane + 128]
                acc = acc * idx[at + 2, j + i].astype(F32) + term
                slots[j + i] = acc.astype(BF)
            return acc

        def body(step, acc):
            for u in range(UNROLL // 4):
                acc = four(step * UNROLL + u * 4, acc)
            return acc

        lax.fori_loop(0, SLOTS // UNROLL, body, jnp.zeros((R, 128), F32))

    def panel_block(rel, which):
        return (((z + rel + 6) % NZ) * 2 + which) * 16

    def share(rel):
        return pl.ds(rel * 16, 16)

    def collect_for_sibling(c, first, count):
        b = bufs[c]

        @pl.loop(0, count)
        def _(o):
            base = panel_block(first + o, 1 - core)
            for i in range(16):
                b["sib_out"][(first + o) * 16 + i] = b["slots"][idx[3, base + i]]

    def send_to_sibling(c, part, first, count):
        b = bufs[c]
        where = pl.ds(first * 16, count * 16)
        remote(b["sib_out"].at[where], b["sib_in"].at[where], sib_send.at[c], sib_recv.at[c, part], sibling)

    def back_project(c):
        b = bufs[c]
        wait_bytes(b["gath"].at[pl.ds(0, 240)], a_recv.at[c])
        tile_sums(b["gath"], b["slots"], 0, False)
        collect_for_sibling(c, 5, 3)
        send_to_sibling(c, 0, 5, 3)
        collect_for_sibling(c, 0, 5)
        send_to_sibling(c, 1, 0, 5)

    def wait_sibling(c, part, first, count):
        where = pl.ds(first * 16, count * 16)
        wait_bytes(bufs[c]["sib_in"].at[where], sib_recv.at[c, part])

    def pair_sum(c, rel, i):
        b = bufs[c]
        own = b["slots"][idx[3, panel_block(rel, core) + i]]
        return own.astype(F32) + b["sib_in"][rel * 16 + i].astype(F32)

    def make_part(c, rel):
        part = bufs[c]["part"]
        for i in range(16):
            part[rel * 16 + i] = pair_sum(c, rel, i).astype(BF)

    def reduce_first(c):
        b = bufs[c]
        wait_sibling(c, 0, 5, 3)
        for rel in (5, 7, 6):
            make_part(c, rel)
        for way, sign, far_rel in ((0, 1, 5), (1, -1, 7)):
            remote(b["part"].at[share(far_rel)], b["far"].at[way], rs_send.at[c], rs_recv.at[c, way], along_z(sign))
            half = pl.ds(6 * 16 + way * 8, 8)
            remote(b["part"].at[half], b["half"].at[way], rs_send.at[c], rs_recv.at[c, 2 + way], along_z(2 * sign))
        wait_sibling(c, 1, 0, 5)
        for way, sign, rel in ((0, 1, 3), (1, -1, 1)):
            make_part(c, rel)
            remote(b["part"].at[share(rel)], b["near"].at[way], rs_send.at[c], rs_recv.at[c, 4 + way], along_z(sign))

    def reduce_second(c):
        b = bufs[c]
        for way, sign, rel in ((0, 1, 4), (1, -1, 0)):
            wait_bytes(b["far"].at[way], rs_recv.at[c, way])
            wait_bytes(b["half"].at[way], rs_recv.at[c, 2 + way])
            for i in range(16):
                total = pair_sum(c, rel, i) + b["far"][way, i].astype(F32)
                if i // 8 == way:
                    total = total + b["half"][way, i % 8].astype(F32)
                b["mid"][way, i] = total.astype(BF)
            remote(b["mid"].at[way], b["mid2"].at[way], rs_send.at[c], rs_recv.at[c, 6 + way], along_z(2 * sign))

    def update(c):
        b = bufs[c]
        for way in range(2):
            wait_bytes(b["near"].at[way], rs_recv.at[c, 4 + way])
            wait_bytes(b["mid2"].at[way], rs_recv.at[c, 6 + way])
        mine = core * 128 + 2 * 16
        for i in range(16):
            total = pair_sum(c, 2, i)
            for way in range(2):
                total = total + b["near"][way, i].astype(F32) + b["mid2"][way, i].astype(F32)
            lanes = slice(i * 128, (i + 1) * 128)
            new = jnp.clip(vol_v[c, :, lanes] + STEP_SIZE * total, 0.0, 1.0)
            newvol[c, :, lanes] = new
            b["vox"][mine + i] = new.astype(BF)
        base = core * 128
        own = b["vox"].at[pl.ds(mine, 16)]
        for n, (dz, rel) in enumerate(((2, 0), (-2, 4), (1, 1), (-1, 3))):
            remote(own, b["vox"].at[pl.ds(base + rel * 16, 16)], ag_send.at[c], ag_recv.at[c, n], along_z(dz))
        pltpu.make_async_copy(newvol.at[c], new_out.at[c], loc_sem.at[c]).start()

    def gather_second(c):
        b = bufs[c]
        base = core * 128
        vox = b["vox"]
        for way, sign, came, goes in ((0, 1, 0, 7), (1, -1, 4, 5)):
            block = vox.at[pl.ds(base + came * 16, 16)]
            wait_bytes(block, ag_recv.at[c, way])
            remote(block, vox.at[pl.ds(base + goes * 16, 16)], ag_send.at[c], ag_recv.at[c, 4 + way], along_z(sign))
            remote(
                vox.at[pl.ds(base + came * 16 + way * 8, 8)], vox.at[pl.ds(base + 6 * 16 + way * 8, 8)],
                ag_send.at[c], ag_recv.at[c, 6 + way], along_z(2 * sign))
        for n, rel in ((2, 1), (3, 3)):
            wait_bytes(vox.at[pl.ds(base + rel * 16, 16)], ag_recv.at[c, n])
        first = vox.at[pl.ds(base, 80)]
        remote(first, first, ag_send.at[c], sib_recv.at[c, 2], sibling)

    def gather_third(c):
        vox = bufs[c]["vox"]
        base = core * 128
        for way, goes in ((0, 7), (1, 5)):
            wait_bytes(vox.at[pl.ds(base + goes * 16, 16)], ag_recv.at[c, 4 + way])
            wait_bytes(vox.at[pl.ds(base + 6 * 16 + way * 8, 8)], ag_recv.at[c, 6 + way])
        last = vox.at[pl.ds(base + 80, 48)]
        remote(last, last, ag_send.at[c], sib_recv.at[c, 3], sibling)

    def project(c):
        b = bufs[c]
        vox, stage, fslots = b["vox"], b["stage"], b["fslots"]
        other = (1 - core) * 128
        wait_bytes(vox.at[pl.ds(other, 80)], sib_recv.at[c, 2])
        wait_bytes(vox.at[pl.ds(other + 80, 48)], sib_recv.at[c, 3])
        tile_sums(vox, fslots, 4, True)

        @pl.loop(0, 32)
        def _(k):
            for j in range(8):
                stage[k, :, j * 128:(j + 1) * 128] = fslots[idx[7, k * 8 + j]]

        @pl.loop(1, PLANE)
        def _(i):
            peer = plane_peer(i)
            remote(stage.at[pl.ds(peer * 2, 2)], proj_out.at[:, a, c], c_send.at[c], c_recv.at[c], {"angle": peer})

        pltpu.make_async_copy(stage.at[pl.ds(a * 2, 2)], proj_out.at[:, a, c], loc_sem.at[NC + c]).start()

    loads[0].wait()
    loads[1].wait()
    misfit_of(0)
    loads[2].wait()
    across_of(0)
    loads[3].wait()
    filter_of(0, 0)
    loads[4].wait()
    loads[5].wait()
    misfit_of(1)
    across_of(1)
    filter_of(0, 1)
    pl.semaphore_wait(barrier, PLANE - 1 + 5)
    send_filtered(0)
    for c in range(1, NC):
        for k in range(2):
            filter_of(c, k)
        send_filtered(c)
    order_tiles()
    loads[6].wait()
    loads[7].wait()

    back_project(0)
    reduce_first(0)
    reduce_second(0)
    back_project(1)
    update(0)
    reduce_first(1)
    gather_second(0)
    reduce_second(1)
    gather_third(0)
    project(0)
    update(1)
    gather_second(1)
    gather_third(1)
    project(1)

    for c in range(NC):
        b = bufs[c]
        wait_bytes(b["filt"].at[pl.ds(0, 240)], a_send.at[c])
        wait_bytes(b["sib_out"], sib_send.at[c])
        wait_bytes(b["vox"].at[pl.ds(0, 112)], rs_send.at[c])
        wait_bytes(b["vox"].at[pl.ds(0, 112 + 128)], ag_send.at[c])
        pltpu.make_async_copy(newvol.at[c], new_out.at[c], loc_sem.at[c]).wait()
        pltpu.make_async_copy(stage_of(b, a), proj_out.at[:, a, c], loc_sem.at[NC + c]).wait()
        wait_bytes(b["stage"].at[pl.ds(0, 30)], c_send.at[c])
        wait_bytes(b["stage"].at[pl.ds(0, 30)], c_recv.at[c])


def stage_of(b, a):
    return b["stage"].at[pl.ds(a * 2, 2)]


def per_device(measured, predicted, slice_filter, column_filter, volume, tiles, tile_ray, tile_vox, live_tiles):
    V = pltpu.VMEM
    D = pltpu.SemaphoreType.DMA
    share = (16, R, 128)
    chunk_scratch = [
        V((256, R, 128), BF),
        V((256, R, 128), BF),
        V((SLOTS + 1, R, 128), BF),
        V((128, R, 128), BF),
        V((128, R, 128), BF),
        V((128, R, 128), BF),
        V((2,) + share, BF),
        V((2,) + share, BF),
        V((2, 8, R, 128), BF),
        V((2,) + share, BF),
        V((2,) + share, BF),
        V((256, R, 128), BF),
        V((SLOTS + 1, R, 128), BF),
        V((32, R, 1024), BF),
    ]
    scratch = [
        V((2, 512, 1024), BF), V((2, 512, 1024), BF), V((PLANE, NC, R, 512), BF), V((1024, 1024), BF),
        V((NC, R, 2048), F32), V((SLOTS, 128, 128), BF), V((512, 1024), BF), V((2, 4, 512, 256), BF),
        V((NC, R, 2048), F32), V((8, 256), I32), V((8, 256), I32), pltpu.SMEM((8, 256), I32),
    ] + chunk_scratch * NC + [
        D((8,)), D, D((NC,)), D((NC,)), D((NC,)), D((NC, 4)), D((NC,)), D((NC, 8)),
        D((NC,)), D((NC, 8)), D((NC,)), D((NC,)), D((2 * NC,)),
    ]
    hbm = pl.BlockSpec(memory_space=pl.ANY)
    vmem = pl.BlockSpec(memory_space=pltpu.VMEM)
    new_share, projected = pl.pallas_call(
        kernel,
        out_shape=(
            jax.ShapeDtypeStruct((NC, R, 2048), F32),
            jax.ShapeDtypeStruct((2, PLANE, NC, R, 1024), BF),
        ),
        in_specs=[hbm] * 6 + [vmem, vmem, pl.BlockSpec(memory_space=pltpu.SMEM)],
        out_specs=(hbm, hbm),
        scratch_shapes=scratch,
        compiler_params=pltpu.CompilerParams(
            collective_id=0, has_side_effects=True, vmem_limit_bytes=60 * 1024 * 1024
        ),
        name="tomography_iteration",
    )(
        measured, predicted, slice_filter.reshape(PLANE, NC, R, 512), column_filter,
        volume.reshape(NC, R, 2048), tiles, tile_ray.reshape(1, SLOTS), tile_vox.reshape(1, SLOTS), live_tiles,
    )
    return new_share.reshape(NC * R, 2048), projected.reshape(2, 512, 1024)


def solution(mesh):
    split = P(("angle", "panel"), None, None)
    return jax.shard_map(
        per_device,
        mesh=mesh,
        in_specs=(
            split, split, P(), P(), P("angle", "panel"), P("panel", None, None), P("panel"), P("panel"), P("panel"),
        ),
        out_specs=(P("angle", "panel"), split),
        check_vma=False,
    )
```

time: 335 us -> 105 us (0.31); the launches traced: 329 us -> 105 us
  waiting for transfers between devices: 124 us -> 0 us
  Pallas kernels: 0 us -> 99 us
  other arithmetic: 73.9 us -> 0 us
  local copies, waits for them, and re-layouts: 47.6 us -> 4.75 us
  blocking collectives: 35.8 us -> 0 us
  matrix products: 25.9 us -> 0 us
  between operations: 14.1 us -> 1.29 us
  starting transfers between devices: 7.72 us -> 0 us
    pallas_call x0 -> x1, Pallas kernels: none -> 99 us  [per_device(): pl.pallas_call(kernel, out_shape=(jax.ShapeDtypeStruct((NC, R, 2048), F32...]
    reduce_scatter x1 -> x0, waiting for transfers between devices: 57.4 us -> none  [per_device(): lax.psum_scatter(gradient.astype(jnp.bfloat16), PANEL, scatter_dimension=...]
    scatter-add x12 -> x0, other arithmetic: 53.2 us -> none  [the longest x6 27.4 us: fore_turn(): summed.at[ray_ids // col_blocks, :, ray_ids % col_blocks, :].add(contrib)]
    all_gather x1 -> x0, waiting for transfers between devices: 35.8 us -> none  [gathered_by_axis(): nearer = lax.all_gather(x, axes[-1], axis=dim, tiled=True)]
    all_to_all x1 -> x0, waiting for transfers between devices: 30.5 us -> none  [per_device(): lax.all_to_all(filtered, 'angle', split_axis=1, concat_axis=0, tiled=True)]
    all_to_all x1 -> x0, blocking collectives: 30.4 us -> none  [per_device(): lax.all_to_all(forward_rays, 'angle', split_axis=0, concat_axis=1, tiled=...]
    gather x12 -> x0, local copies, waits for them, and re-layouts: 26.7 us -> none  [the longest x6 13.5 us: back_turn(): picked = ray_grid[ray_ids // col_blocks, :, ray_ids % col_blocks, :]]
    dot_general x14 -> x0, matrix products: 25.9 us -> none  [the longest x6 11.3 us: fore_turn(): jnp.einsum('stv,trv->tsr', picked, tile_piece, preferred_element_type=jnp...]
  transfers between devices with their start and end apart: 3 -> 0, of which waited for: 3 -> 0; matrix products, arithmetic and copies ran while one was open for 0% -> 0% of each run, Pallas kernels for 0% -> 0%
where the time goes in v1:
time: 105 us
  Pallas kernels  99 us (94%)
  local copies, waits for them, and re-layouts  4.75 us (5%)
  between operations  1.29 us (1%)
    pallas_call x1, Pallas kernels, per_device(): pl.pallas_call(kernel, out_shape=(jax.ShapeDtypeStruct((NC, R, 2048), F32...  99 us
    unnamed x2, local copies, waits for them, and re-layouts  4.75 us

profile of v1, /device:TPU:1, one launch (start us, length us, event | category | flops | bytes accessed | tf_op | source)
XLA Modules:
  0.0 105.1 jit_solution(14449094812726530544)
XLA Ops:
  1.3 99.0 %tomography_iteration.1 = (f32[2,16,2048]{2,1,0:T(8,128)}, bf16[2,16,2,16,1024]{4,3,2,1,0:T(8,128)(2,1)}) custom-call(bf16[2,512,1024]{2,1,0:T(8,128)(2,1)} %measured.1, bf16[2,512,1024]{2,1,0:T(8,128)(2,1)} %predicted.1, bf16[16,2,16,512]{3,2,1,0:T(8,128)(2,1)} %bitcast.7, bf16[1024,1024]{1,0:T(8,128)(2,1)} %cfilt.1, f32[2,16,2048]{2,1,0:T(8,128)} %bitcast.8, ...), custom_call_target="tpu_custom_call" | custom-call | tf_op jit(solution)/shard_map/tomography_iteration/pallas_call | solution.py:406
  100.3 1.7 %copy.14 = f32[32,2048]{1,0:T(8,128)} copy(f32[32,2048]{1,0:T(8,128)} %bitcast.9) | data formatting | bytes 524288
  102.0 3.1 %copy.15 = bf16[2,512,1024]{2,1,0:T(8,128)(2,1)} copy(bf16[2,512,1024]{2,1,0:T(8,128)(2,1)} %bitcast.6) | data formatting | bytes 4194304

commit v2 on v1

--- a/solution.py
+++ b/solution.py
@@ -14,17 +14,24 @@
 PLANE = 16
 NZ = 8
 SLOTS = 192
-UNROLL = 32
+UNROLL = 96
 STEP_SIZE = 0.1
-NC = 2
-R = 32 // NC
+ACROSS_UNROLL = 2
+SPLIT_ANGLES = True
+UNIT = 8
+UNITS = (1, 1, 1, 1)
+NC = len(UNITS)
+SCHEDULE = (
+    "B0 10 B1 20", "11 U0 B2 21", "12 30 U1 B3", "22 40 13 31", "U2 23 P0 32", "41 U3 P1 42", "33 P2 43 P3",
+)
+FIRST = tuple(sum(UNITS[:c]) for c in range(NC))
 
 
 def kernel(
-    measured, predicted, sfilt, cfilt, volume, tiles_hbm, ray_ref, vox_ref, live_ref,
+    measured, predicted, sfilt, cfilt, volume, tiles_hbm, ray_hbm, vox_hbm, live_ref,
     new_out, proj_out,
     m_v, p_v, sf_v, cf_v, vol_v, tiles, misfit, across, newvol,
-    keys, idx_v, idx, *rest,
+    keys, ray_v, vox_v, idx_v, idx, *rest,
 ):
     names = (
         "filt", "gath", "slots", "sib_out", "sib_in", "part", "near", "far", "half", "mid", "mid2",
@@ -47,16 +54,26 @@
     def along_z(dz):
         return {"panel": ((z + dz + NZ) % NZ) * 2 + core}
 
+    def units_of(c):
+        return pl.ds(FIRST[c], UNITS[c])
+
+    def volume_store(c):
+        return pltpu.make_async_copy(newvol.at[units_of(c)], new_out.at[units_of(c)], loc_sem.at[c])
+
+    def own_projection(c):
+        return pltpu.make_async_copy(
+            bufs[c]["stage"].at[pl.ds(a * 2, 2)], proj_out.at[:, a, units_of(c)], loc_sem.at[NC + c])
+
     sibling = {"panel": z * 2 + (1 - core)}
 
     loads = [
         pltpu.make_async_copy(src, dst, in_sem.at[i])
         for i, (src, dst) in enumerate((
             (predicted.at[0], p_v.at[0]), (measured.at[0], m_v.at[0]), (cfilt, cf_v), (sfilt, sf_v),
-            (predicted.at[1], p_v.at[1]), (measured.at[1], m_v.at[1]), (tiles_hbm, tiles), (volume, vol_v),
+            (predicted.at[1], p_v.at[1]), (measured.at[1], m_v.at[1]), (tiles_hbm, tiles), (volume, vol_v), (ray_hbm, ray_v), (vox_hbm, vox_v),
         ))
     ]
-    for load in loads:
+    for load in loads[:6]:
         load.start()
 
     barrier = pltpu.get_barrier_semaphore()
@@ -76,36 +93,38 @@
             misfit[rows, :] = ((m_v[k, rows, :].astype(F32) - bright) * bright).astype(BF)
 
     def across_of(k):
-        @pl.loop(0, 4)
-        def _(n):
-            columns = pl.ds(pl.multiple_of(n * 256, 256), 256)
-            across[k, n] = jnp.dot(misfit[...], cf_v[:, columns], preferred_element_type=F32).astype(BF)
+        @pl.loop(0, 4 // ACROSS_UNROLL)
+        def _(step):
+            for u in range(ACROSS_UNROLL):
+                n = step * ACROSS_UNROLL + u
+                columns = pl.ds(pl.multiple_of(n * 256, 256), 256)
+                across[k, n] = jnp.dot(misfit[...], cf_v[:, columns], preferred_element_type=F32).astype(BF)
 
     def filter_of(c, k):
         filt = bufs[c]["filt"]
-
-        @pl.loop(0, 4)
-        def _(n):
-            rows = sf_v[:, c].reshape(PLANE * R, 512)
+        r = UNITS[c] * UNIT
+
+        rows = sf_v[:, FIRST[c]:FIRST[c] + UNITS[c]].reshape(PLANE * r, 512)
+        for n in range(4):
             out = jnp.dot(rows, across[k, n], preferred_element_type=F32).astype(BF)
             for d in range(PLANE):
                 for j in range(2):
-                    filt[d * 16 + k * 8 + n * 2 + j] = out[d * R:(d + 1) * R, j * 128:(j + 1) * 128]
-
-    def send_filtered(c):
+                    filt[d * 16 + k * 8 + n * 2 + j] = out[d * r:(d + 1) * r, j * 128:(j + 1) * 128]
+
+    def send_filtered(c, at=0, count=16):
         filt, gath = bufs[c]["filt"], bufs[c]["gath"]
 
         @pl.loop(1, PLANE)
         def _(i):
             peer = plane_peer(i)
             pltpu.make_async_remote_copy(
-                src_ref=filt.at[pl.ds(peer * 16, 16)],
-                dst_ref=gath.at[pl.ds(a * 16, 16)],
+                src_ref=filt.at[pl.ds(peer * 16 + at, count)],
+                dst_ref=gath.at[pl.ds(a * 16 + at, count)],
                 send_sem=a_send.at[c], recv_sem=a_recv.at[c],
                 device_id={"angle": peer}, device_id_type=MESH,
             ).start()
 
-        gath[pl.ds(a * 16, 16)] = filt[pl.ds(a * 16, 16)]
+        gath[pl.ds(a * 16 + at, count)] = filt[pl.ds(a * 16 + at, count)]
 
     def wait_bytes(ref, sem):
         pltpu.make_async_copy(ref, ref, sem).wait()
@@ -120,8 +139,8 @@
         col = lax.broadcasted_iota(I32, (256, 256), 1)
         dead = 256
         keys[...] = jnp.full((8, 256), dead, I32)
-        keys[0:1, 0:SLOTS] = vox_ref[...]
-        keys[1:2, 0:SLOTS] = ray_ref[...]
+        keys[0:1, 0:SLOTS] = vox_v[...]
+        keys[1:2, 0:SLOTS] = ray_v[...]
         live = live_ref[0]
 
         def down(x):
@@ -157,9 +176,10 @@
         move.start()
         move.wait()
 
-    def tile_sums(source, slots, at, transposed):
-        slots[SLOTS] = jnp.zeros((R, 128), BF)
-        blank = jnp.zeros((R, 128), BF)
+    def tile_sums(c, source, slots, at, transposed):
+        r = UNITS[c] * UNIT
+        blank = jnp.zeros((r, 128), BF)
+        slots[SLOTS] = blank
         joined = 0 if transposed else 1
         contract = (((1,), (1,)), ((), ())) if transposed else (((1,), (0,)), ((), ()))
 
@@ -174,7 +194,7 @@
             out = lax.dot_general(left, right, contract, preferred_element_type=F32)
             for i in range(4):
                 lane = (i % 2) * 128
-                term = out[i * R:(i + 1) * R, lane:lane + 128]
+                term = out[i * r:(i + 1) * r, lane:lane + 128]
                 acc = acc * idx[at + 2, j + i].astype(F32) + term
                 slots[j + i] = acc.astype(BF)
             return acc
@@ -184,7 +204,7 @@
                 acc = four(step * UNROLL + u * 4, acc)
             return acc
 
-        lax.fori_loop(0, SLOTS // UNROLL, body, jnp.zeros((R, 128), F32))
+        lax.fori_loop(0, SLOTS // UNROLL, body, jnp.zeros((r, 128), F32))
 
     def panel_block(rel, which):
         return (((z + rel + 6) % NZ) * 2 + which) * 16
@@ -209,7 +229,7 @@
     def back_project(c):
         b = bufs[c]
         wait_bytes(b["gath"].at[pl.ds(0, 240)], a_recv.at[c])
-        tile_sums(b["gath"], b["slots"], 0, False)
+        tile_sums(c, b["gath"], b["slots"], 0, False)
         collect_for_sibling(c, 5, 3)
         send_to_sibling(c, 0, 5, 3)
         collect_for_sibling(c, 0, 5)
@@ -266,14 +286,15 @@
             for way in range(2):
                 total = total + b["near"][way, i].astype(F32) + b["mid2"][way, i].astype(F32)
             lanes = slice(i * 128, (i + 1) * 128)
-            new = jnp.clip(vol_v[c, :, lanes] + STEP_SIZE * total, 0.0, 1.0)
-            newvol[c, :, lanes] = new
+            old = vol_v[units_of(c), :, lanes].reshape(UNITS[c] * UNIT, 128)
+            new = jnp.clip(old + STEP_SIZE * total, 0.0, 1.0)
+            newvol[units_of(c), :, lanes] = new.reshape(UNITS[c], UNIT, 128)
             b["vox"][mine + i] = new.astype(BF)
         base = core * 128
         own = b["vox"].at[pl.ds(mine, 16)]
         for n, (dz, rel) in enumerate(((2, 0), (-2, 4), (1, 1), (-1, 3))):
             remote(own, b["vox"].at[pl.ds(base + rel * 16, 16)], ag_send.at[c], ag_recv.at[c, n], along_z(dz))
-        pltpu.make_async_copy(newvol.at[c], new_out.at[c], loc_sem.at[c]).start()
+        volume_store(c).start()
 
     def gather_second(c):
         b = bufs[c]
@@ -306,56 +327,58 @@
         other = (1 - core) * 128
         wait_bytes(vox.at[pl.ds(other, 80)], sib_recv.at[c, 2])
         wait_bytes(vox.at[pl.ds(other + 80, 48)], sib_recv.at[c, 3])
-        tile_sums(vox, fslots, 4, True)
+        tile_sums(c, vox, fslots, 4, True)
 
         @pl.loop(0, 32)
         def _(k):
             for j in range(8):
-                stage[k, :, j * 128:(j + 1) * 128] = fslots[idx[7, k * 8 + j]]
+                block = fslots[idx[7, k * 8 + j]]
+                stage[k, :, :, j * 128:(j + 1) * 128] = block.reshape(UNITS[c], UNIT, 128)
 
         @pl.loop(1, PLANE)
         def _(i):
             peer = plane_peer(i)
-            remote(stage.at[pl.ds(peer * 2, 2)], proj_out.at[:, a, c], c_send.at[c], c_recv.at[c], {"angle": peer})
-
-        pltpu.make_async_copy(stage.at[pl.ds(a * 2, 2)], proj_out.at[:, a, c], loc_sem.at[NC + c]).start()
-
-    loads[0].wait()
-    loads[1].wait()
+            remote(stage.at[pl.ds(peer * 2, 2)], proj_out.at[:, a, units_of(c)], c_send.at[c], c_recv.at[c], {"angle": peer})
+
+        own_projection(c).start()
+
+    for load in loads[:2]:
+        load.wait()
     misfit_of(0)
     loads[2].wait()
     across_of(0)
     loads[3].wait()
+    for load in loads[6:]:
+        load.start()
     filter_of(0, 0)
-    loads[4].wait()
-    loads[5].wait()
+    pl.semaphore_wait(barrier, PLANE - 1 + 5)
+    if SPLIT_ANGLES:
+        send_filtered(0, 0, 8)
+    for load in loads[4:6]:
+        load.wait()
     misfit_of(1)
     across_of(1)
     filter_of(0, 1)
-    pl.semaphore_wait(barrier, PLANE - 1 + 5)
-    send_filtered(0)
+    if SPLIT_ANGLES:
+        send_filtered(0, 8, 8)
+    else:
+        send_filtered(0)
     for c in range(1, NC):
         for k in range(2):
             filter_of(c, k)
         send_filtered(c)
+    for load in loads[8:]:
+        load.wait()
     order_tiles()
-    loads[6].wait()
-    loads[7].wait()
-
-    back_project(0)
-    reduce_first(0)
-    reduce_second(0)
-    back_project(1)
-    update(0)
-    reduce_first(1)
-    gather_second(0)
-    reduce_second(1)
-    gather_third(0)
-    project(0)
-    update(1)
-    gather_second(1)
-    gather_third(1)
-    project(1)
+    for load in loads[6:8]:
+        load.wait()
+
+    stages = {
+        "B": back_project, "1": reduce_first, "2": reduce_second, "U": update, "3": gather_second,
+        "4": gather_third, "P": project,
+    }
+    for step in " ".join(SCHEDULE).split():
+        stages[step[0]](int(step[1]))
 
     for c in range(NC):
         b = bufs[c]
@@ -363,64 +386,62 @@
         wait_bytes(b["sib_out"], sib_send.at[c])
         wait_bytes(b["vox"].at[pl.ds(0, 112)], rs_send.at[c])
         wait_bytes(b["vox"].at[pl.ds(0, 112 + 128)], ag_send.at[c])
-        pltpu.make_async_copy(newvol.at[c], new_out.at[c], loc_sem.at[c]).wait()
-        pltpu.make_async_copy(stage_of(b, a), proj_out.at[:, a, c], loc_sem.at[NC + c]).wait()
+        volume_store(c).wait()
+        own_projection(c).wait()
         wait_bytes(b["stage"].at[pl.ds(0, 30)], c_send.at[c])
         wait_bytes(b["stage"].at[pl.ds(0, 30)], c_recv.at[c])
-
-
-def stage_of(b, a):
-    return b["stage"].at[pl.ds(a * 2, 2)]
 
 
 def per_device(measured, predicted, slice_filter, column_filter, volume, tiles, tile_ray, tile_vox, live_tiles):
     V = pltpu.VMEM
     D = pltpu.SemaphoreType.DMA
-    share = (16, R, 128)
-    chunk_scratch = [
-        V((256, R, 128), BF),
-        V((256, R, 128), BF),
-        V((SLOTS + 1, R, 128), BF),
-        V((128, R, 128), BF),
-        V((128, R, 128), BF),
-        V((128, R, 128), BF),
-        V((2,) + share, BF),
-        V((2,) + share, BF),
-        V((2, 8, R, 128), BF),
-        V((2,) + share, BF),
-        V((2,) + share, BF),
-        V((256, R, 128), BF),
-        V((SLOTS + 1, R, 128), BF),
-        V((32, R, 1024), BF),
-    ]
+    chunks = []
+    for u in UNITS:
+        r = u * UNIT
+        share = (16, r, 128)
+        chunks += [
+            V((256, r, 128), BF),
+            V((256, r, 128), BF),
+            V((SLOTS + 1, r, 128), BF),
+            V((128, r, 128), BF),
+            V((128, r, 128), BF),
+            V((128, r, 128), BF),
+            V((2,) + share, BF),
+            V((2,) + share, BF),
+            V((2, 8, r, 128), BF),
+            V((2,) + share, BF),
+            V((2,) + share, BF),
+            V((256, r, 128), BF),
+            V((SLOTS + 1, r, 128), BF),
+            V((32, u, UNIT, 1024), BF),
+        ]
     scratch = [
-        V((2, 512, 1024), BF), V((2, 512, 1024), BF), V((PLANE, NC, R, 512), BF), V((1024, 1024), BF),
-        V((NC, R, 2048), F32), V((SLOTS, 128, 128), BF), V((512, 1024), BF), V((2, 4, 512, 256), BF),
-        V((NC, R, 2048), F32), V((8, 256), I32), V((8, 256), I32), pltpu.SMEM((8, 256), I32),
-    ] + chunk_scratch * NC + [
-        D((8,)), D, D((NC,)), D((NC,)), D((NC,)), D((NC, 4)), D((NC,)), D((NC, 8)),
+        V((2, 512, 1024), BF), V((2, 512, 1024), BF), V((PLANE, 4, UNIT, 512), BF), V((1024, 1024), BF),
+        V((4, UNIT, 2048), F32), V((SLOTS, 128, 128), BF), V((512, 1024), BF), V((2, 4, 512, 256), BF),
+        V((4, UNIT, 2048), F32), V((8, 256), I32), V((1, SLOTS), I32), V((1, SLOTS), I32), V((8, 256), I32), pltpu.SMEM((8, 256), I32),
+    ] + chunks + [
+        D((10,)), D, D((NC,)), D((NC,)), D((NC,)), D((NC, 4)), D((NC,)), D((NC, 8)),
         D((NC,)), D((NC, 8)), D((NC,)), D((NC,)), D((2 * NC,)),
     ]
-    hbm = pl.BlockSpec(memory_space=pl.ANY)
-    vmem = pl.BlockSpec(memory_space=pltpu.VMEM)
+    anywhere = pl.BlockSpec(memory_space=pl.ANY)
     new_share, projected = pl.pallas_call(
         kernel,
         out_shape=(
-            jax.ShapeDtypeStruct((NC, R, 2048), F32),
-            jax.ShapeDtypeStruct((2, PLANE, NC, R, 1024), BF),
+            jax.ShapeDtypeStruct((4, UNIT, 2048), F32),
+            jax.ShapeDtypeStruct((2, PLANE, 4, UNIT, 1024), BF),
         ),
-        in_specs=[hbm] * 6 + [vmem, vmem, pl.BlockSpec(memory_space=pltpu.SMEM)],
-        out_specs=(hbm, hbm),
+        in_specs=[pl.BlockSpec(memory_space=pltpu.HBM)] * 8 + [pl.BlockSpec(memory_space=pltpu.SMEM)],
+        out_specs=(anywhere, anywhere),
         scratch_shapes=scratch,
         compiler_params=pltpu.CompilerParams(
-            collective_id=0, has_side_effects=True, vmem_limit_bytes=60 * 1024 * 1024
+            collective_id=0, has_side_effects=True, vmem_limit_bytes=36 * 1024 * 1024
         ),
         name="tomography_iteration",
-    )(
-        measured, predicted, slice_filter.reshape(PLANE, NC, R, 512), column_filter,
-        volume.reshape(NC, R, 2048), tiles, tile_ray.reshape(1, SLOTS), tile_vox.reshape(1, SLOTS), live_tiles,
-    )
-    return new_share.reshape(NC * R, 2048), projected.reshape(2, 512, 1024)
+    )(*[pltpu.with_memory_space_constraint(x, pltpu.HBM) for x in (
+        measured, predicted, slice_filter.reshape(PLANE, 4, UNIT, 512), column_filter,
+        volume.reshape(4, UNIT, 2048), tiles, tile_ray.reshape(1, SLOTS), tile_vox.reshape(1, SLOTS),
+    )], live_tiles)
+    return new_share.reshape(32, 2048), projected.reshape(2, 512, 1024)
 
 
 def solution(mesh):

time: 105 us -> 80.9 us (0.77)
  Pallas kernels: 99 us -> 77.4 us
  local copies, waits for them, and re-layouts: 4.75 us -> 2.02 us
    pallas_call x1, Pallas kernels: 99 us -> 77.4 us  [per_device(): pl.pallas_call(kernel, out_shape=(jax.ShapeDtypeStruct((4, UNIT, 2048), F...]
    unnamed x2, local copies, waits for them, and re-layouts: 4.75 us -> 2.02 us
where the time goes in v2:
time: 80.9 us; the launch traced here: 80.7 us
  Pallas kernels  77.4 us (96%)
  local copies, waits for them, and re-layouts  2.02 us (2%)
  between operations  1.29 us (2%)
    pallas_call x1, Pallas kernels, per_device(): pl.pallas_call(kernel, out_shape=(jax.ShapeDtypeStruct((4, UNIT, 2048), F...  77.4 us
    unnamed x2, local copies, waits for them, and re-layouts  2.02 us

profile of v2, /device:TPU:1, one launch (start us, length us, event | category | flops | bytes accessed | tf_op | source)
XLA Modules:
  0.0 80.7 jit_solution(7850204253484168005)
XLA Ops:
  1.3 77.4 %tomography_iteration.1 = (f32[4,8,2048]{2,1,0:T(8,128)S(1)}, bf16[2,16,4,8,1024]{4,3,2,1,0:T(8,128)(2,1)S(1)}) custom-call(bf16[2,512,1024]{2,1,0:T(8,128)(2,1)} %measured.1, bf16[2,512,1024]{2,1,0:T(8,128)(2,1)} %predicted.1, bf16[16,4,8,512]{3,2,1,0:T(8,128)(2,1)} %bitcast.8, bf16[1024,1024]{1,0:T(8,128)(2,1)} %cfilt.1, f32[4,8,2048]{2,1,0:T(8,128)} %bitcast.9, ...), custom_call_target="tpu_custom_call" | custom-call | tf_op jit(solution)/shard_map/tomography_iteration/pallas_call | solution.py:427
  78.7 0.7 copy.14
  79.4 1.3 %copy.15 = bf16[2,512,1024]{2,1,0:T(8,128)(2,1)} copy(bf16[2,512,1024]{2,1,0:T(8,128)(2,1)S(1)} %bitcast.6) | data formatting | bytes 4194304

commit v3 on v2

--- a/solution.py
+++ b/solution.py
@@ -16,13 +16,11 @@
 SLOTS = 192
 UNROLL = 96
 STEP_SIZE = 0.1
-ACROSS_UNROLL = 2
-SPLIT_ANGLES = True
 UNIT = 8
 UNITS = (1, 1, 1, 1)
 NC = len(UNITS)
 SCHEDULE = (
-    "B0 10 B1 20", "11 U0 B2 21", "12 30 U1 B3", "22 40 13 31", "U2 23 P0 32", "41 U3 P1 42", "33 P2 43 P3",
+    "F1 O0 F2 B0", "10 F3 B1 20", "11 U0 B2 21", "12 30 U1 B3", "22 40 13 31", "U2 23 P0 32", "41 U3 P1 42", "33 P2 43 P3",
 )
 FIRST = tuple(sum(UNITS[:c]) for c in range(NC))
 
@@ -73,7 +71,7 @@
             (predicted.at[1], p_v.at[1]), (measured.at[1], m_v.at[1]), (tiles_hbm, tiles), (volume, vol_v), (ray_hbm, ray_v), (vox_hbm, vox_v),
         ))
     ]
-    for load in loads[:6]:
+    for load in loads[:3]:
         load.start()
 
     barrier = pltpu.get_barrier_semaphore()
@@ -85,20 +83,23 @@
     for peer in (sibling, along_z(1), along_z(-1), along_z(2), along_z(-2)):
         pl.semaphore_signal(barrier, inc=1, device_id=peer, device_id_type=MESH)
 
+    def misfit_rows(k, rows):
+        bright = jnp.exp(-p_v[k, rows, :].astype(F32))
+        misfit[k, rows, :] = ((m_v[k, rows, :].astype(F32) - bright) * bright).astype(BF)
+
     def misfit_of(k):
-        @pl.loop(0, 8)
+        @pl.loop(0, 4)
         def _(i):
-            rows = pl.ds(pl.multiple_of(i * 64, 64), 64)
-            bright = jnp.exp(-p_v[k, rows, :].astype(F32))
-            misfit[rows, :] = ((m_v[k, rows, :].astype(F32) - bright) * bright).astype(BF)
-
-    def across_of(k):
-        @pl.loop(0, 4 // ACROSS_UNROLL)
-        def _(step):
-            for u in range(ACROSS_UNROLL):
-                n = step * ACROSS_UNROLL + u
-                columns = pl.ds(pl.multiple_of(n * 256, 256), 256)
-                across[k, n] = jnp.dot(misfit[...], cf_v[:, columns], preferred_element_type=F32).astype(BF)
+            for u in range(2):
+                misfit_rows(k, pl.ds(pl.multiple_of(i * 128 + u * 64, 64), 64))
+
+    def across_of(k, tiles_of_columns, beside=None):
+        for n in tiles_of_columns:
+            if beside is not None:
+                for v in range(4):
+                    misfit_rows(beside, pl.ds((n - 2) * 256 + v * 64, 64))
+            columns = pl.ds(n * 256, 256)
+            across[k, n] = jnp.dot(misfit[k], cf_v[:, columns], preferred_element_type=F32).astype(BF)
 
     def filter_of(c, k):
         filt = bufs[c]["filt"]
@@ -344,38 +345,38 @@
 
     for load in loads[:2]:
         load.wait()
+    for load in loads[3:6]:
+        load.start()
     misfit_of(0)
     loads[2].wait()
-    across_of(0)
-    loads[3].wait()
+    across_of(0, (0, 1))
+    for load in loads[3:6]:
+        load.wait()
     for load in loads[6:]:
         load.start()
+    across_of(0, (2, 3), 1)
     filter_of(0, 0)
     pl.semaphore_wait(barrier, PLANE - 1 + 5)
-    if SPLIT_ANGLES:
-        send_filtered(0, 0, 8)
-    for load in loads[4:6]:
-        load.wait()
-    misfit_of(1)
-    across_of(1)
+    send_filtered(0, 0, 8)
+    across_of(1, range(4))
     filter_of(0, 1)
-    if SPLIT_ANGLES:
-        send_filtered(0, 8, 8)
-    else:
-        send_filtered(0)
-    for c in range(1, NC):
+    send_filtered(0, 8, 8)
+
+    def filter_chunk(c):
         for k in range(2):
             filter_of(c, k)
         send_filtered(c)
-    for load in loads[8:]:
-        load.wait()
-    order_tiles()
-    for load in loads[6:8]:
-        load.wait()
+
+    def order_step(_):
+        for load in loads[8:]:
+            load.wait()
+        order_tiles()
+        for load in loads[6:8]:
+            load.wait()
 
     stages = {
         "B": back_project, "1": reduce_first, "2": reduce_second, "U": update, "3": gather_second,
-        "4": gather_third, "P": project,
+        "4": gather_third, "P": project, "F": filter_chunk, "O": order_step,
     }
     for step in " ".join(SCHEDULE).split():
         stages[step[0]](int(step[1]))
@@ -390,6 +391,30 @@
         own_projection(c).wait()
         wait_bytes(b["stage"].at[pl.ds(0, 30)], c_send.at[c])
         wait_bytes(b["stage"].at[pl.ds(0, 30)], c_recv.at[c])
+
+
+def store_kernel(share, projected, share_out, projected_out, sem):
+    copies = []
+    for i in range(8):
+        at = i // 4, pl.ds((i % 4) * 128, 128)
+        copies.append(pltpu.make_async_copy(projected.at[at], projected_out.at[at], sem.at[i]))
+    copies.append(pltpu.make_async_copy(share, share_out, sem.at[8]))
+    for copy in copies:
+        copy.start()
+    for copy in copies:
+        copy.wait()
+
+
+def stored(share, projected):
+    return pl.pallas_call(
+        store_kernel,
+        out_shape=(
+            jax.ShapeDtypeStruct(share.shape, share.dtype), jax.ShapeDtypeStruct(projected.shape, projected.dtype)),
+        in_specs=[pl.BlockSpec(memory_space=pl.ANY)] * 2,
+        out_specs=(pl.BlockSpec(memory_space=pltpu.HBM), pl.BlockSpec(memory_space=pltpu.HBM)),
+        scratch_shapes=[pltpu.SemaphoreType.DMA((9,))],
+        name="store_results",
+    )(*[pltpu.with_memory_space_constraint(x, pltpu.VMEM) for x in (share, projected)])
 
 
 def per_device(measured, predicted, slice_filter, column_filter, volume, tiles, tile_ray, tile_vox, live_tiles):
@@ -417,7 +442,7 @@
         ]
     scratch = [
         V((2, 512, 1024), BF), V((2, 512, 1024), BF), V((PLANE, 4, UNIT, 512), BF), V((1024, 1024), BF),
-        V((4, UNIT, 2048), F32), V((SLOTS, 128, 128), BF), V((512, 1024), BF), V((2, 4, 512, 256), BF),
+        V((4, UNIT, 2048), F32), V((SLOTS, 128, 128), BF), V((2, 512, 1024), BF), V((2, 4, 512, 256), BF),
         V((4, UNIT, 2048), F32), V((8, 256), I32), V((1, SLOTS), I32), V((1, SLOTS), I32), V((8, 256), I32), pltpu.SMEM((8, 256), I32),
     ] + chunks + [
         D((10,)), D, D((NC,)), D((NC,)), D((NC,)), D((NC, 4)), D((NC,)), D((NC, 8)),
@@ -441,7 +466,7 @@
         measured, predicted, slice_filter.reshape(PLANE, 4, UNIT, 512), column_filter,
         volume.reshape(4, UNIT, 2048), tiles, tile_ray.reshape(1, SLOTS), tile_vox.reshape(1, SLOTS),
     )], live_tiles)
-    return new_share.reshape(32, 2048), projected.reshape(2, 512, 1024)
+    return stored(new_share.reshape(32, 2048), projected.reshape(2, 512, 1024))
 
 
 def solution(mesh):

time: 80.9 us -> 80.7 us (level)
  local copies, waits for them, and re-layouts: 2.02 us -> 0 us
  Pallas kernels: 77.4 us -> 79.4 us
    unnamed x2 -> x0, local copies, waits for them, and re-layouts: 2.02 us -> none
    pallas_call x0 -> x1, Pallas kernels: none -> 1.47 us  [stored(): pl.pallas_call(store_kernel, out_shape=(jax.ShapeDtypeStruct(share.shape,...]
where the time goes in v3:
time: 80.7 us; the launch traced here: 80.6 us
  Pallas kernels  79.4 us (98%)
  between operations  1.29 us (2%)
    pallas_call x1, Pallas kernels, per_device(): pl.pallas_call(kernel, out_shape=(jax.ShapeDtypeStruct((4, UNIT, 2048), F...  77.9 us

profile of v3, /device:TPU:1, one launch (start us, length us, event | category | flops | bytes accessed | tf_op | source)
XLA Modules:
  0.0 80.6 jit_solution(13688581918509713555)
XLA Ops:
  1.3 77.9 %tomography_iteration.1 = (f32[4,8,2048]{2,1,0:T(8,128)S(1)}, bf16[2,16,4,8,1024]{4,3,2,1,0:T(8,128)(2,1)S(1)}) custom-call(bf16[2,512,1024]{2,1,0:T(8,128)(2,1)} %measured.1, bf16[2,512,1024]{2,1,0:T(8,128)(2,1)} %predicted.1, bf16[16,4,8,512]{3,2,1,0:T(8,128)(2,1)} %bitcast.8, bf16[1024,1024]{1,0:T(8,128)(2,1)} %cfilt.1, f32[4,8,2048]{2,1,0:T(8,128)} %bitcast.9, ...), custom_call_target="tpu_custom_call" | custom-call | tf_op jit(solution)/shard_map/tomography_iteration/pallas_call | solution.py:452
  79.2 1.5 %store_results.1 = (f32[32,2048]{1,0:T(8,128)}, bf16[2,512,1024]{2,1,0:T(8,128)(2,1)}) custom-call(f32[32,2048]{1,0:T(8,128)S(1)} %bitcast.7, bf16[2,512,1024]{2,1,0:T(8,128)(2,1)S(1)} %bitcast.6), custom_call_target="tpu_custom_call" | custom-call | tf_op jit(solution)/shard_map/store_results/pallas_call | solution.py:409
